TPU v7x, 256 devices: a whole 4x4x8 slice. The times are simulated.
256 devices in a mesh: rows: 128 (over x_lo, y, z, core), cols: 2 (over x_hi).
Axes of the slice: x: 4 (x_hi: 2, x_lo: 2; x = x_hi * 2 + x_lo), y: 4, z: 8, core: 2. Of those that a mesh axis runs over, the one named last changes fastest.
Arguments:
- features: bfloat16 [32768, 128], P('rows', 'cols'), may hold values from -6 to 6
- adj_tiles: bfloat16 [12288, 128, 128], P('rows'), may hold values from -0.109375 to 0.109375
- tile_src: int32 [12288], P('rows'), may hold values from 0 to 255, as said below
- tile_dst: int32 [12288], P('rows'), may hold values from 0 to 1, as said below
- tile_count: int32 [128], P('rows'), may hold values from 24 to 96, as said below
- cluster_size: int32 [256], P('rows'), may hold values from 64 to 128, as said below
- weight: bfloat16 [128, 256], P(None, 'cols'), may hold values from -0.5 to 0.5
- bias: float32 [256], P('cols'), may hold values from -3 to 3
- grad_out: bfloat16 [32768, 256], P('rows', 'cols'), may hold values from -6 to 6
Outputs:
- hidden: bfloat16 [32768, 256], P('rows', 'cols')
- grad_weight: float32 [128, 256], P(None, 'cols')
- grad_bias: float32 [256], P('cols')
- grad_features: bfloat16 [32768, 128], P('rows', 'cols')
Inputs may be any that keep to these rules, and one draw needn't show every extreme that they name: In row group r, slots 0 to tile_count[r] - 1 of its 96 slots hold tiles, in non-decreasing order of tile_src; the later slots are unused: their tile_src and tile_dst hold 0, and their adj_tiles hold arbitrary values that must not contribute. A used slot's column cluster belongs to row group r itself or to a row group whose index differs from r in exactly one bit (row group g holds clusters g * 2 to g * 2 + 1). Equal (row, column) pairs may repeat and then add. `tile_dst`: unused slots hold 0. `tile_count`: some row groups use all 96 slots. `cluster_size`: the real nodes of a cluster are its first ones; some cluster is full.
All inputs are finite; a program needn't handle non-finite values.
Results may differ from a plain program's by a relative error of at most 0.006.
Values may be sent and summed in bfloat16 or wider, within the bound.
A program may use at most 64 MiB of HBM per device.

v0:
```python
import math
import jax
import jax.numpy as jnp
from jax import lax
from jax.sharding import PartitionSpec as P

TILE_GROUP = 16


def sweep_slots(first_slot, last_slot, work, totals):
    turn_count = (last_slot - first_slot + TILE_GROUP - 1) // TILE_GROUP

    def one_turn(turn_index, carried):
        slot_ids = first_slot + turn_index * TILE_GROUP + jnp.arange(TILE_GROUP, dtype=jnp.int32)
        return work(carried, slot_ids, slot_ids < last_slot)

    return lax.fori_loop(0, jnp.maximum(turn_count, 0), one_turn, totals)


def slot_bounds(sources, first_slot, last_slot, low_cluster, high_cluster):
    positions = jnp.arange(sources.shape[0], dtype=jnp.int32)
    inside = (positions >= first_slot) & (positions < last_slot)
    below_low = jnp.sum((inside & (sources < low_cluster)).astype(jnp.int32))
    below_high = jnp.sum((inside & (sources < high_cluster)).astype(jnp.int32))
    return (first_slot + below_low, first_slot + below_high)


def gather_products(
    totals, tile_data, sources, targets, slot_ids, is_valid, row_table, base_cluster
):
    clamped = jnp.minimum(slot_ids, tile_data.shape[0] - 1)
    tile_block = tile_data[clamped]
    from_rows = jnp.clip(sources[clamped] - base_cluster, 0, row_table.shape[0] - 1)
    products = jnp.einsum(
        "tij,tjf->tif", tile_block, row_table[from_rows], preferred_element_type=jnp.float32
    )
    placed = jnp.where(is_valid, targets[clamped], totals.shape[0])
    return totals.at[placed].add(products, mode="drop")


def spread_products(totals, tile_data, sources, targets, slot_ids, is_valid, grad_table):
    clamped = jnp.minimum(slot_ids, tile_data.shape[0] - 1)
    tile_block = tile_data[clamped]
    products = jnp.einsum(
        "tji,tjf->tif", tile_block, grad_table[targets[clamped]], preferred_element_type=jnp.float32
    )
    placed = jnp.where(is_valid, sources[clamped], totals.shape[0])
    return totals.at[placed].add(products, mode="drop")


def local(
    features, adj_tiles, tile_src, tile_dst, tile_count, cluster_size, weight, bias, grad_out
):
    clusters_here = cluster_size.shape[0]
    tile_width = adj_tiles.shape[1]
    feat_half = features.shape[1]
    node_rows = clusters_here * tile_width
    node_ids = jnp.arange(tile_width, dtype=jnp.int32)
    live_node = (node_ids[None, :] < cluster_size[:, None]).astype(jnp.float32)[:, :, None]
    live_flat = live_node.reshape(node_rows, 1)
    masked = (
        features.reshape(clusters_here, tile_width, feat_half).astype(jnp.float32) * live_node
    ).astype(jnp.bfloat16)
    my_count = tile_count[0]
    zero_totals = jnp.zeros((clusters_here, tile_width, feat_half), jnp.float32)
    whole_rows = lax.all_gather(masked, "rows", axis=0, tiled=True)
    row_count = whole_rows.shape[0]
    first_slot, last_slot = slot_bounds(tile_src, 0, my_count, 0, 0 + row_count)
    own_totals = sweep_slots(
        first_slot,
        last_slot,
        lambda totals, slot_ids, is_valid: gather_products(
            totals, adj_tiles, tile_src, tile_dst, slot_ids, is_valid, whole_rows, 0
        ),
        zero_totals,
    )
    agg_local = own_totals.reshape(node_rows, feat_half).astype(jnp.bfloat16)
    agg_full = lax.all_gather(agg_local, "cols", axis=1, tiled=True)
    pre_activation = jnp.dot(agg_full, weight, preferred_element_type=jnp.float32) + bias
    sigmoid_pre = jax.nn.sigmoid(pre_activation)
    hidden = (pre_activation * sigmoid_pre * live_flat).astype(jnp.bfloat16)
    grad_pre = (
        grad_out.astype(jnp.float32)
        * sigmoid_pre
        * (1.0 + pre_activation * (1.0 - sigmoid_pre))
        * live_flat
    ).astype(jnp.bfloat16)
    weight_term = lax.dot_general(
        agg_full, grad_pre, (((0,), (0,)), ((), ())), preferred_element_type=jnp.float32
    )
    bias_term = jnp.sum(grad_pre.astype(jnp.float32), axis=0)
    weight_total, bias_total = lax.psum((weight_term, bias_term), "rows")
    grad_scale = 1.0 / math.sqrt(node_rows * lax.axis_size("rows"))
    grad_weight = weight_total * grad_scale
    grad_bias = bias_total * grad_scale
    partial_value = lax.dot_general(
        grad_pre, weight, (((1,), (1,)), ((), ())), preferred_element_type=jnp.float32
    )
    grad_agg = (
        lax.psum_scatter(partial_value, "cols", scatter_dimension=1, tiled=True)
        .astype(jnp.bfloat16)
        .reshape(clusters_here, tile_width, feat_half)
    )
    start_row = jnp.int32(0)
    totals = jnp.zeros((clusters_here * lax.axis_size("rows"), tile_width, feat_half), jnp.float32)
    first_slot, last_slot = slot_bounds(
        tile_src, 0, my_count, start_row, start_row + clusters_here * lax.axis_size("rows")
    )
    summed = lax.psum_scatter(
        sweep_slots(
            first_slot,
            last_slot,
            lambda carried, slot_ids, is_valid: spread_products(
                carried, adj_tiles, tile_src, tile_dst, slot_ids, is_valid, grad_agg
            ),
            totals,
        ),
        "rows",
        scatter_dimension=0,
        tiled=True,
    )
    grad_features = (summed * live_node).reshape(node_rows, feat_half).astype(jnp.bfloat16)
    return (hidden, grad_weight, grad_bias, grad_features)


def solution(mesh):
    return jax.shard_map(
        local,
        mesh=mesh,
        in_specs=(
            P("rows", "cols"),
            P("rows", None, None),
            P("rows"),
            P("rows"),
            P("rows"),
            P("rows"),
            P(None, "cols"),
            P("cols"),
            P("rows", "cols"),
        ),
        out_specs=(P("rows", "cols"), P(None, "cols"), P("cols"), P("rows", "cols")),
        check_vma=False,
    )
```

profile of v0, /device:TPU:4, one launch (start us, length us, event | category | flops | bytes accessed | tf_op | source)
XLA Modules:
  0.0 1835.9 jit_solution(9324555501634384926)
XLA Ops:
  7.2 0.7 fusion.9
  8.0 0.8 reshape.169
  8.8 0.6 copy.26
  10.1 1.4 fusion.8
  12.8 216.2 %all-gather.2.cloned.1.call-done = bf16[256,128,64]{1,2,0:T(8,128)(2,1)} async-done(((bf16[2,128,64]{1,2,0:T(8,128)(2,1)}), bf16[256,128,64]{1,2,0:T(8,128)(2,1)}) %all-gather.2.cloned.1.call-update) | async-done | bytes 4194320 | tf_op jit(solution)/shard_map/all_gather | solution.py:66
  229.0 8.4 copy.27
  237.4 33.4 %while.20 = (s32[]{:T(128)}, f32[2,128,64]{1,2,0:T(8,128)S(1)}, s32[]{:T(128)}, s32[]{:T(128)}, s32[]{:T(128)}, /*index=5*/s32[96]{0:T(128)S(1)}, bf16[96,128,12...) while((s32[]{:T(128)}, f32[2,128,64]{1,2,0:T(8,128)S(1)}, ...), condition=%wide.region_4.5_spmd, body=%wide.region_2.4_spmd.sunk | while | flops 33687796 | bytes 4465809 | solution.py:17
  238.1 0.7 gather_fusion.2
  238.7 0.7 gather_fusion
  239.4 0.7 fusion.39
  240.1 4.0 gather_fusion.3
  244.1 2.5 gather_fusion.1
  246.7 0.5 fusion.41
  247.2 1.4 scatter_fusion
  249.2 0.7 gather_fusion.2
  249.8 0.7 gather_fusion
  250.5 0.7 fusion.39
  251.2 4.0 gather_fusion.3
  255.3 2.5 gather_fusion.1
  257.8 0.5 fusion.41
  258.3 1.4 scatter_fusion
  260.3 0.7 gather_fusion.2
  261.0 0.7 gather_fusion
  261.6 0.7 fusion.39
  262.3 4.0 gather_fusion.3
  266.4 2.5 gather_fusion.1
  268.9 0.5 fusion.41
  269.4 1.4 scatter_fusion
  270.8 6.1 all_gather.7
  276.9 0.9 convert_reduce_fusion
  277.8 0.8 fusion.13
  278.7 0.8 fusion.12
  279.5 44.7 %reduce-scatter.3.cloned.1.call-done = f32[256,64]{0,1:T(8,128)} async-done(((f32[256,128]{0,1:T(8,128)}), f32[256,64]{0,1:T(8,128)}) %reduce-scatter.3.cloned.1.call-update) | async-done | bytes 65552 | tf_op jit(solution)/shard_map/reduce_scatter | solution.py:100
  324.2 0.8 convert_element_type.74
  325.2 4.3 broadcast_in_dim.17
  329.5 26.7 %while.21 = (s32[]{:T(128)}, f32[256,128,64]{1,2,0:T(8,128)}, s32[]{:T(128)}, s32[]{:T(128)}, s32[]{:T(128)}, /*index=5*/s32[96]{0:T(128)S(1)}, bf16[96,128,128]...) while((s32[]{:T(128)}, f32[256,128,64]{1,2,0:T(8,128)}, ...), condition=%wide.region_11.12_spmd, body=%wide.region_9.11_spmd.sunk | while | flops 33687780 | bytes 4465809 | solution.py:17
  330.1 0.7 gather_fusion.6
  330.8 0.7 gather_fusion.4
  331.5 0.7 fusion.45
  332.2 0.6 gather_fusion.7
  332.8 2.5 gather_fusion.5
  335.4 0.3 fusion.47
  335.7 2.7 scatter_fusion.1
  339.0 0.7 gather_fusion.6
  339.6 0.7 gather_fusion.4
  340.3 0.7 fusion.45
  341.0 0.6 gather_fusion.7
  341.7 2.5 gather_fusion.5
  344.2 0.3 fusion.47
  344.5 2.7 scatter_fusion.1
  347.9 0.7 gather_fusion.6
  348.6 0.7 gather_fusion.4
  349.2 0.7 fusion.45
  349.9 0.6 gather_fusion.7
  350.6 2.5 gather_fusion.5
  353.1 0.3 fusion.47
  353.5 2.7 scatter_fusion.1
  356.2 299.2 %psum.15 = f32[128]{0:T(128)S(1)} all-reduce(f32[128]{0:T(128)S(1)} %get-tuple-element.194), channel_id=1, replica_groups=mesh['rows'=128,'cols'=2] {'rows'}, use_global_device_ids=true, to_apply=%region_7.8 | all-reduce | flops 128 | bytes 1024 | tf_op jit(solution)/shard_map/psum | solution.py:92
  655.4 0.5 broadcast_multiply_fusion.1
  656.0 599.3 %all-reduce.2.cloned.1.call-done = f32[128,128]{1,0:T(8,128)} async-done(((f32[128,128]{1,0:T(8,128)}), f32[128,128]{1,0:T(8,128)}) %all-reduce.2.cloned.1.call-update) | async-done | bytes 65552 | tf_op jit(solution)/shard_map/psum | solution.py:92
  1255.2 1.5 broadcast_multiply_fusion
  1256.7 571.1 %reduce-scatter.5.cloned.1.call-done = f32[2,128,64]{1,2,0:T(8,128)} async-done(((f32[256,128,64]{1,2,0:T(8,128)}), f32[2,128,64]{1,2,0:T(8,128)}) %reduce-scatter.5.cloned.1.call-update) | async-done | bytes 65552 | tf_op jit(solution)/shard_map/reduce_scatter | solution.py:109
  1827.8 0.9 fusion.6
  1828.7 0.6 copy.41
  (46 shorter events, 0.6 us)
Async XLA Ops:
  7.2 269.7 %copy-start = (bf16[128,128]{1,0:T(8,128)(2,1)S(1)}, bf16[128,128]{1,0:T(8,128)(2,1)}, u32[]{:S(2)}) copy-start(bf16[128,128]{1,0:T(8,128)(2,1)} %param.19) | copy-start | bytes 98308
  7.2 230.2 %copy-start.1 = (s32[96]{0:T(128)S(1)}, s32[96]{0:T(128)}, u32[]{:S(2)}) copy-start(s32[96]{0:T(128)} %param.15) | copy-start | bytes 1156
  7.2 230.2 %copy-start.2 = (s32[96]{0:T(128)S(1)}, s32[96]{0:T(128)}, u32[]{:S(2)}) copy-start(s32[96]{0:T(128)} %param.16) | copy-start | bytes 1156
  7.2 221.8 %all-gather.2.cloned.1.call-start = ((), (), s32[]{:S(2)}) async-start(), calls=%async_computation.2 | async-start | bytes 4227072 | tf_op jit(solution)/shard_map/all_gather | solution.py:66
  9.4 314.8 %reduce-scatter.3.cloned.1.call-start = ((), (), s32[]{:S(2)}) async-start(), calls=%async_computation.4 | async-start | bytes 196608 | tf_op jit(solution)/shard_map/reduce_scatter | solution.py:100
  237.4 39.5 %copy-start.3 = (bf16[256,128]{1,0:T(8,128)(2,1)S(1)}, bf16[256,128]{1,0:T(8,128)(2,1)}, u32[]{:S(2)}) copy-start(bf16[256,128]{1,0:T(8,128)(2,1)} %param.21) | copy-start | bytes 196612
  237.4 39.5 %copy-start.4 = (f32[128]{0:T(128)S(1)}, f32[128]{0:T(128)}, u32[]{:S(2)}) copy-start(f32[128]{0:T(128)} %param.20) | copy-start | bytes 1540
  278.6 976.6 %all-reduce.2.cloned.1.call-start = ((), (), s32[]{:S(2)}) async-start(), calls=%async_computation.3 | async-start | bytes 131072 | tf_op jit(solution)/shard_map/psum | solution.py:92
  279.5 1548.4 %reduce-scatter.5.cloned.1.call-start = ((), (), s32[]{:S(2)}) async-start(), calls=%async_computation.5 | async-start | bytes 8454144 | tf_op jit(solution)/shard_map/reduce_scatter | solution.py:109
Sparse Core Ops, SparseCore 0:
  10.5 218.4 all-gather.1
  278.7 45.4 reduce-scatter.2
  327.4 927.7 all-reduce.1
  1257.7 570.0 reduce-scatter.4
where the time goes:
time: 1840 us
  waiting for transfers between devices  1430 us (78%)
  blocking collectives  305 us (17%)
  local copies, waits for them, and re-layouts  52 us (3%)
  other arithmetic  22.3 us (1%)
    psum x1, waiting for transfers between devices, local(): weight_total, bias_total = lax.psum((weight_term, bias_term), 'rows')  599 us
    reduce_scatter x1, waiting for transfers between devices, local(): lax.psum_scatter(sweep_slots(first_slot, last_slot, lambda carried, slot_...  571 us
    psum x1, blocking collectives, local(): weight_total, bias_total = lax.psum((weight_term, bias_term), 'rows')  299 us
    all_gather x1, waiting for transfers between devices, local(): whole_rows = lax.all_gather(masked, 'rows', axis=0, tiled=True)  216 us
    reduce_scatter x1, waiting for transfers between devices, local(): lax.psum_scatter(partial_value, 'cols', scatter_dimension=1, tiled=True)  44.7 us
  transfers between devices with their start and end apart: 4, of which 4 were waited for; matrix products, arithmetic and copies ran while one was open for 2% of the time, Pallas kernels for 0%

commit v1 on v0

--- a/solution.py
+++ b/solution.py
@@ -5,6 +5,9 @@
 from jax.sharding import PartitionSpec as P
 
 TILE_GROUP = 16
+_perform_widths = lambda in_array: jnp.concatenate(
+    lax.all_to_all(jnp.stack([in_array] * lax.psum(1, "rows")), "rows", 0, 0), axis=0
+)
 
 
 def sweep_slots(first_slot, last_slot, work, totals):
@@ -63,7 +66,7 @@
     ).astype(jnp.bfloat16)
     my_count = tile_count[0]
     zero_totals = jnp.zeros((clusters_here, tile_width, feat_half), jnp.float32)
-    whole_rows = lax.all_gather(masked, "rows", axis=0, tiled=True)
+    whole_rows = _perform_widths(masked)
     row_count = whole_rows.shape[0]
     first_slot, last_slot = slot_bounds(tile_src, 0, my_count, 0, 0 + row_count)
     own_totals = sweep_slots(

time: 1840 us -> 1710 us (0.929)
  waiting for transfers between devices: 1430 us -> 1290 us
    all_gather x1 -> x0, waiting for transfers between devices: 216 us -> none  [local(): whole_rows = lax.all_gather(masked, 'rows', axis=0, tiled=True)]
    all_to_all x0 -> x1, waiting for transfers between devices: none -> 92.9 us  [lax.all_to_all(jnp.stack([in_array] * lax.psum(1, 'rows')), 'rows', 0, 0)]
where the time goes in v1:
time: 1710 us
  waiting for transfers between devices  1290 us (75%)
  blocking collectives  305 us (18%)
  local copies, waits for them, and re-layouts  54.4 us (3%)
  other arithmetic  21.7 us (1%)
  between operations  17.5 us (1%)
    psum x1, waiting for transfers between devices, local(): weight_total, bias_total = lax.psum((weight_term, bias_term), 'rows')  582 us
    reduce_scatter x1, waiting for transfers between devices, local(): lax.psum_scatter(sweep_slots(first_slot, last_slot, lambda carried, slot_...  569 us
    psum x1, blocking collectives, local(): weight_total, bias_total = lax.psum((weight_term, bias_term), 'rows')  299 us
    all_to_all x1, waiting for transfers between devices, lax.all_to_all(jnp.stack([in_array] * lax.psum(1, 'rows')), 'rows', 0, 0)  92.9 us
    reduce_scatter x1, waiting for transfers between devices, local(): lax.psum_scatter(partial_value, 'cols', scatter_dimension=1, tiled=True)  44.2 us
  transfers between devices with their start and end apart: 4, of which 4 were waited for; matrix products, arithmetic and copies ran while one was open for 2% of the time, Pallas kernels for 0%

profile of v1, /device:TPU:4, one launch (start us, length us, event | category | flops | bytes accessed | tf_op | source)
XLA Modules:
  0.0 1710.5 jit_solution(3245245534850392063)
XLA Ops:
  8.0 0.7 fusion.9
  8.8 0.8 reshape.176
  9.6 3.0 stack.2
  12.6 14.5 all-to-all-start
  27.8 0.7 fusion.8
  29.8 92.9 %all-to-all-done = bf16[128,2,128,64]{2,3,1,0:T(8,128)(2,1)} async-done(((bf16[128,2,128,64]{2,3,1,0:T(8,128)(2,1)}), bf16[128,2,128,64]{2,3,1,0:T(8,128)(2,1)}, u32[]{:S(2)}, u32[]{:S(2)}) %all-to-all-start) | async-done | bytes 4194336 | tf_op jit(solution)/shard_map/all_to_all | solution.py:9
  122.8 8.4 copy.27
  131.2 33.4 %while.20 = (s32[]{:T(128)}, f32[2,128,64]{1,2,0:T(8,128)S(1)}, s32[]{:T(128)}, s32[]{:T(128)}, s32[]{:T(128)}, /*index=5*/s32[96]{0:T(128)S(1)}, bf16[96,128,12...) while((s32[]{:T(128)}, f32[2,128,64]{1,2,0:T(8,128)S(1)}, ...), condition=%wide.region_4.5_spmd, body=%wide.region_2.4_spmd.sunk | while | flops 33687796 | bytes 4465809 | solution.py:20
  131.8 0.7 gather_fusion.2
  132.5 0.7 gather_fusion
  133.2 0.7 fusion.39
  133.9 4.0 gather_fusion.3
  137.9 2.5 gather_fusion.1
  140.5 0.5 fusion.41
  140.9 1.4 scatter_fusion
  142.9 0.7 gather_fusion.2
  143.6 0.7 gather_fusion
  144.3 0.7 fusion.39
  145.0 4.0 gather_fusion.3
  149.0 2.5 gather_fusion.1
  151.6 0.5 fusion.41
  152.0 1.4 scatter_fusion
  154.1 0.7 gather_fusion.2
  154.7 0.7 gather_fusion
  155.4 0.7 fusion.39
  156.1 4.0 gather_fusion.3
  160.1 2.5 gather_fusion.1
  162.7 0.5 fusion.41
  163.2 1.4 scatter_fusion
  164.5 6.1 all_gather.3
  170.7 0.9 convert_reduce_fusion
  171.5 0.8 fusion.13
  172.4 0.8 fusion.12
  173.3 44.2 %reduce-scatter.3.cloned.1.call-done = f32[256,64]{0,1:T(8,128)} async-done(((f32[256,128]{0,1:T(8,128)}), f32[256,64]{0,1:T(8,128)}) %reduce-scatter.3.cloned.1.call-update) | async-done | bytes 65552 | tf_op jit(solution)/shard_map/reduce_scatter | solution.py:103
  217.5 0.8 convert_element_type.78
  218.5 4.3 broadcast_in_dim.17
  222.8 26.7 %while.21 = (s32[]{:T(128)}, f32[256,128,64]{1,2,0:T(8,128)}, s32[]{:T(128)}, s32[]{:T(128)}, s32[]{:T(128)}, /*index=5*/s32[96]{0:T(128)S(1)}, bf16[96,128,128]...) while((s32[]{:T(128)}, f32[256,128,64]{1,2,0:T(8,128)}, ...), condition=%wide.region_11.12_spmd, body=%wide.region_9.11_spmd.sunk | while | flops 33687780 | bytes 4465809 | solution.py:20
  223.4 0.7 gather_fusion.6
  224.1 0.7 gather_fusion.4
  224.7 0.7 fusion.45
  225.4 0.6 gather_fusion.7
  226.1 2.6 gather_fusion.5
  228.7 0.3 fusion.47
  229.0 2.7 scatter_fusion.1
  232.3 0.7 gather_fusion.6
  232.9 0.7 gather_fusion.4
  233.6 0.7 fusion.45
  234.3 0.6 gather_fusion.7
  235.0 2.6 gather_fusion.5
  237.5 0.3 fusion.47
  237.8 2.7 scatter_fusion.1
  241.2 0.7 gather_fusion.6
  241.9 0.7 gather_fusion.4
  242.5 0.7 fusion.45
  243.2 0.6 gather_fusion.7
  243.9 2.5 gather_fusion.5
  246.8 2.7 scatter_fusion.1
  249.5 299.2 %psum.15 = f32[128]{0:T(128)S(1)} all-reduce(f32[128]{0:T(128)S(1)} %get-tuple-element.176), channel_id=1, replica_groups=mesh['rows'=128,'cols'=2] {'rows'}, use_global_device_ids=true, to_apply=%region_7.8 | all-reduce | flops 128 | bytes 1024 | tf_op jit(solution)/shard_map/psum | solution.py:95
  548.7 0.5 broadcast_multiply_fusion.1
  549.2 581.8 %all-reduce.2.cloned.1.call-done = f32[128,128]{1,0:T(8,128)} async-done(((f32[128,128]{1,0:T(8,128)}), f32[128,128]{1,0:T(8,128)}) %all-reduce.2.cloned.1.call-update) | async-done | bytes 65552 | tf_op jit(solution)/shard_map/psum | solution.py:95
  1131.1 1.5 broadcast_multiply_fusion
  1132.5 569.1 %reduce-scatter.5.cloned.1.call-done = f32[2,128,64]{1,2,0:T(8,128)} async-done(((f32[256,128,64]{1,2,0:T(8,128)}), f32[2,128,64]{1,2,0:T(8,128)}) %reduce-scatter.5.cloned.1.call-update) | async-done | bytes 65552 | tf_op jit(solution)/shard_map/reduce_scatter | solution.py:112
  1701.6 0.9 fusion.6
  1702.5 0.6 copy.41
  (46 shorter events, 0.8 us)
Async XLA Ops:
  8.0 162.6 %copy-start = (bf16[128,128]{1,0:T(8,128)(2,1)S(1)}, bf16[128,128]{1,0:T(8,128)(2,1)}, u32[]{:S(2)}) copy-start(bf16[128,128]{1,0:T(8,128)(2,1)} %param.19) | copy-start | bytes 98308
  8.0 19.8 %copy-start.1 = (s32[96]{0:T(128)S(1)}, s32[96]{0:T(128)}, u32[]{:S(2)}) copy-start(s32[96]{0:T(128)} %param.15) | copy-start | bytes 1156
  12.6 110.2 %all-to-all-start = ((bf16[128,2,128,64]{2,3,1,0:T(8,128)(2,1)}), bf16[128,2,128,64]{2,3,1,0:T(8,128)(2,1)}, u32[]{:S(2)}, u32[]{:S(2)}) async-start(bf16[128,2,128,64]{2,3,1,0:T(8,128)(2,1)} %stack.2), calls=%async_computation | async-start | bytes 8388608 | tf_op jit(solution)/shard_map/all_to_all | solution.py:9
  27.1 104.0 %copy-start.2 = (s32[96]{0:T(128)S(1)}, s32[96]{0:T(128)}, u32[]{:S(2)}) copy-start(s32[96]{0:T(128)} %param.16) | copy-start | bytes 1156
  27.1 190.4 %reduce-scatter.3.cloned.1.call-start = ((), (), s32[]{:S(2)}) async-start(), calls=%async_computation.4 | async-start | bytes 196608 | tf_op jit(solution)/shard_map/reduce_scatter | solution.py:103
  131.1 39.5 %copy-start.3 = (bf16[256,128]{1,0:T(8,128)(2,1)S(1)}, bf16[256,128]{1,0:T(8,128)(2,1)}, u32[]{:S(2)}) copy-start(bf16[256,128]{1,0:T(8,128)(2,1)} %param.21) | copy-start | bytes 196612
  131.2 39.5 %copy-start.4 = (f32[128]{0:T(128)S(1)}, f32[128]{0:T(128)}, u32[]{:S(2)}) copy-start(f32[128]{0:T(128)} %param.20) | copy-start | bytes 1540
  172.4 958.7 %all-reduce.2.cloned.1.call-start = ((), (), s32[]{:S(2)}) async-start(), calls=%async_computation.3 | async-start | bytes 131072 | tf_op jit(solution)/shard_map/psum | solution.py:95
  173.2 1528.4 %reduce-scatter.5.cloned.1.call-start = ((), (), s32[]{:S(2)}) async-start(), calls=%async_computation.5 | async-start | bytes 8454144 | tf_op jit(solution)/shard_map/reduce_scatter | solution.py:112
Sparse Core Ops, SparseCore 0:
  172.5 44.9 reduce-scatter.2
Sparse Core Ops, SparseCore 1:
  176.0 955.0 all-reduce.1
  1133.6 567.9 reduce-scatter.4
